TPU v7x, 512 devices: a whole 4x4x16 slice. The times are simulated.
512 devices in a mesh: tm: 64 (over z, x_hi, core), mic: 8 (over x_lo, y).
Axes of the slice: x: 4 (x_hi: 2, x_lo: 2; x = x_hi * 2 + x_lo), y: 4, z: 16, core: 2. Of those that a mesh axis runs over, the one named last changes fastest.
Arguments:
- signal: bfloat16 [262144, 4096], P('tm', 'mic')
- mic_pos: int32 [3, 4096], P(None, 'mic'), may hold values from 0 to 255, as said below
- grid_pos: int32 [3, 8192], replicated, may hold values from 0 to 255, as said below
- bins: int32 [2], replicated, may hold values from 1 to 511, as said below
Outputs:
- power: float32 [8192], P('mic')
Inputs may be any that keep to these rules, and one draw needn't show every extreme that they name: `mic_pos`: rows are x, y, z; a microphone's z is below 16. `grid_pos`: rows are x, y, z; a grid point's z is 64 or more and below 128. `bins`: the bin indices are distinct; the first is 511.
All inputs are finite; a program needn't handle non-finite values.
Results may differ from a plain program's by a relative error of at most 0.0006.
The roundings to bfloat16 on the way count: a program that leaves them out, or rounds other values in their place, can miss the bound.
Values may be sent and summed in bfloat16 or wider, within the bound.
A program may use at most 64 MiB of HBM per device.

v0:
```python
import math

import jax
import jax.numpy as jnp
from jax import lax
from jax.sharding import PartitionSpec as P

MICS = 4096
SEGLEN = 8192
NBINS = 2


def from_behind(shard, axis, by):
    size = lax.axis_size(axis)
    pairs = [(i, i + by) for i in range(size) if 0 <= i + by < size]
    return lax.ppermute(shard, axis, pairs)


def fourier_rows(bins):
    sample_index = jnp.arange(SEGLEN, dtype=jnp.int32)
    window = 0.5 - 0.5 * jnp.cos(2.0 * math.pi * sample_index.astype(jnp.float32) / SEGLEN)
    phases = bins[:, None] * sample_index[None, :] % SEGLEN
    angles = 2.0 * math.pi * phases.astype(jnp.float32) / SEGLEN
    weighting = window / math.sqrt(0.375 * SEGLEN)
    fourier = jnp.stack([weighting * jnp.cos(angles), -weighting * jnp.sin(angles)], axis=1)
    return fourier.reshape(2 * NBINS, SEGLEN).astype(jnp.bfloat16)


def steer_block(points, mic_pos, bins):
    offsets = points[:, :, None] - mic_pos[:, None, :]
    distance = jnp.sqrt(jnp.sum(offsets * offsets, axis=0).astype(jnp.float32))
    strength = 16.0 / distance
    cycles = bins.astype(jnp.float32)[:, None, None] * distance[None] * (16.0 / SEGLEN)
    cosine_part = (strength[None] * jnp.cos(2.0 * math.pi * cycles)).astype(jnp.bfloat16)
    sine_part = (strength[None] * jnp.sin(2.0 * math.pi * cycles)).astype(jnp.bfloat16)
    return (cosine_part, sine_part)


def steered(spectra, cosine_part, sine_part):
    segments = spectra.shape[0]
    mic_count = spectra.shape[2]
    width = cosine_part.shape[1]
    per_bin = []
    for bin_index in range(NBINS):
        bin_pair = spectra[:, 2 * bin_index : 2 * bin_index + 2, :].reshape(2 * segments, mic_count)
        cosine_sum = jnp.dot(
            bin_pair, cosine_part[bin_index].T, preferred_element_type=jnp.float32
        ).reshape(segments, 2, width)
        sine_sum = jnp.dot(
            bin_pair, sine_part[bin_index].T, preferred_element_type=jnp.float32
        ).reshape(segments, 2, width)
        real_part = cosine_sum[:, 0] - sine_sum[:, 1]
        imag_part = cosine_sum[:, 1] + sine_sum[:, 0]
        per_bin.append(jnp.stack([real_part, imag_part], axis=1))
    return jnp.stack(per_bin, axis=1)


def beams_for(spectra, chosen_points, mic_pos, bins):
    point_count = chosen_points.shape[1]
    block_width = min(point_count, 1024)
    block_count = point_count // block_width
    points = chosen_points.reshape(3, block_count, block_width).transpose(1, 0, 2)

    def block_beam(block_points):
        cosine_part, sine_part = steer_block(block_points, mic_pos, bins)
        return steered(spectra, cosine_part, sine_part)

    partial_value = lax.map(block_beam, points)
    segments = spectra.shape[0]
    return partial_value.transpose(1, 2, 3, 0, 4).reshape(segments, NBINS, 2, point_count)


def local(signal, mic_pos, grid_pos, bins):
    fourier = fourier_rows(bins)
    following = from_behind(signal, "tm", -1)
    segment = jnp.concatenate([signal, following], axis=0)
    spectrum = jnp.dot(fourier, segment, preferred_element_type=jnp.float32)
    spectrum = spectrum.astype(jnp.bfloat16)
    grid_count = grid_pos.shape[1]
    owners = lax.axis_size("mic")
    owned_count = grid_count // owners
    spans = lax.axis_size("tm")
    partial_value = beams_for(spectrum[None], grid_pos, mic_pos, bins)[0]
    summed = lax.psum(partial_value, "mic")
    owned = lax.dynamic_slice_in_dim(summed, lax.axis_index("mic") * owned_count, owned_count, 2)
    local_power = jnp.sum(owned * owned, axis=(0, 1))
    power_sum = lax.psum(local_power, "tm")
    return power_sum / (spans * NBINS * MICS)


def solution(mesh):
    in_specs = (P("tm", "mic"), P(None, "mic"), P(), P())
    out_specs = P("mic")
    return jax.shard_map(local, mesh=mesh, in_specs=in_specs, out_specs=out_specs, check_vma=False)
```

profile of v0, /device:TPU:1, one launch (start us, length us, event | category | flops | bytes accessed | tf_op | source)
XLA Modules:
  0.0 457.2 jit_solution(10412396298532731741)
XLA Ops:
  6.5 8.8 %collective-permute-start = (bf16[4096,512]{1,0:T(8,128)(2,1)}, bf16[4096,512]{1,0:T(8,128)(2,1)}, u32[]{:S(2)}, u32[]{:S(2)}) collective-permute-start(bf16[4096,512]{1,0:T(8,128)(2,1)} %param.6), channel_id=1, source_target_pairs={{8,0},{16,8},{24,16},{32,24},{40,32},{48,40},{56,48},{64,56},{72,6... | collective-permute-start | bytes 12582920 | tf_op jit(solution)/shard_map/ppermute | solution.py:16
  15.5 1.9 multiply_convert_fusion.3
  18.3 40.8 %collective-permute-done = bf16[4096,512]{1,0:T(8,128)(2,1)} collective-permute-done((bf16[4096,512]{1,0:T(8,128)(2,1)}, bf16[4096,512]{1,0:T(8,128)(2,1)}, u32[]{:S(2)}, u32[]{:S(2)}) %collective-permute-start) | collective-permute-done | bytes 4194336 | tf_op jit(solution)/shard_map/ppermute | solution.py:16
  59.1 4.6 %fusion.16 = bf16[1,4,512]{2,1,0:T(4,128)(2,1)S(1)} fusion(bf16[4,8192]{1,0:T(4,128)(2,1)S(1)} %convert_element_type.74, bf16[4096,512]{1,0:T(8,128)(2,1)} %collective-permute-done, bf16[4096,512]{1,0:T(8,128)(2,1)} %param.6), kind=kOutput, calls=%fused_computation.36 | convolution fusion | flops 50333696 | bytes 8458240 | tf_op jit(solution)/shard_map/dot_general | solution.py:77
  63.7 161.1 %while.12 = (s32[]{:T(128)}, f32[8,1,2,2,1024]{4,3,2,1,0:T(2,128)S(1)}, s32[8,3,1024]{2,1,0:T(4,128)}, s32[3,512]{1,0:T(4,128)S(1)}, f32[2,1,1]{0,2,1:T(1,128)S(1)}, /*index=5*/bf16[1,4,512]{2,1,0:T(4,128)(2,1)S(1)}, s32[]{:T(128)}) while((s32[]{:T(128)}, f32[8,1,2,2,1024]{4,3,2,1,0:T(2,128)S(1)}, s32[8,3,1024]{2,1,0:T(4,128)}, ...), condition=%wide.region_2.3_spmd, body=%wide.region_0.2_spmd.sunk | while | flops 19935232 | bytes 21170268 | solution.py:68
  64.5 0.9 multiply_reduce_fusion.3
  66.1 16.1 %multiply_convert_fusion.5 = (bf16[2,1024,512]{2,1,0:T(8,128)(2,1)S(1)}, bf16[2,1024,512]{2,1,0:T(8,128)(2,1)S(1)}) fusion(f32[1024,512]{1,0:T(8,128)S(1)} %get-tuple-element.158, f32[2]{0:T(128)S(1)} %bitcast.94, f32[1024,512]{1,0:T(8,128)S(1)} %get-tuple-element.159), kind=kLoop, calls=%fused_computation.2.clone.1 | loop fusion | flops 6291456 | bytes 8388616 | tf_op jit(solution)/shard_map/while/body/eval_jaxpr/convert_element_type | solution.py:34
  84.6 0.9 multiply_reduce_fusion.3
  86.2 16.1 %multiply_convert_fusion.5 = (bf16[2,1024,512]{2,1,0:T(8,128)(2,1)S(1)}, bf16[2,1024,512]{2,1,0:T(8,128)(2,1)S(1)}) fusion(f32[1024,512]{1,0:T(8,128)S(1)} %get-tuple-element.158, f32[2]{0:T(128)S(1)} %bitcast.94, f32[1024,512]{1,0:T(8,128)S(1)} %get-tuple-element.159), kind=kLoop, calls=%fused_computation.2.clone.1 | loop fusion | flops 6291456 | bytes 8388616 | tf_op jit(solution)/shard_map/while/body/eval_jaxpr/convert_element_type | solution.py:34
  104.7 0.9 multiply_reduce_fusion.3
  106.4 16.1 %multiply_convert_fusion.5 = (bf16[2,1024,512]{2,1,0:T(8,128)(2,1)S(1)}, bf16[2,1024,512]{2,1,0:T(8,128)(2,1)S(1)}) fusion(f32[1024,512]{1,0:T(8,128)S(1)} %get-tuple-element.158, f32[2]{0:T(128)S(1)} %bitcast.94, f32[1024,512]{1,0:T(8,128)S(1)} %get-tuple-element.159), kind=kLoop, calls=%fused_computation.2.clone.1 | loop fusion | flops 6291456 | bytes 8388616 | tf_op jit(solution)/shard_map/while/body/eval_jaxpr/convert_element_type | solution.py:34
  124.9 0.9 multiply_reduce_fusion.3
  126.5 16.1 %multiply_convert_fusion.5 = (bf16[2,1024,512]{2,1,0:T(8,128)(2,1)S(1)}, bf16[2,1024,512]{2,1,0:T(8,128)(2,1)S(1)}) fusion(f32[1024,512]{1,0:T(8,128)S(1)} %get-tuple-element.158, f32[2]{0:T(128)S(1)} %bitcast.94, f32[1024,512]{1,0:T(8,128)S(1)} %get-tuple-element.159), kind=kLoop, calls=%fused_computation.2.clone.1 | loop fusion | flops 6291456 | bytes 8388616 | tf_op jit(solution)/shard_map/while/body/eval_jaxpr/convert_element_type | solution.py:34
  145.0 0.9 multiply_reduce_fusion.3
  146.6 16.1 %multiply_convert_fusion.5 = (bf16[2,1024,512]{2,1,0:T(8,128)(2,1)S(1)}, bf16[2,1024,512]{2,1,0:T(8,128)(2,1)S(1)}) fusion(f32[1024,512]{1,0:T(8,128)S(1)} %get-tuple-element.158, f32[2]{0:T(128)S(1)} %bitcast.94, f32[1024,512]{1,0:T(8,128)S(1)} %get-tuple-element.159), kind=kLoop, calls=%fused_computation.2.clone.1 | loop fusion | flops 6291456 | bytes 8388616 | tf_op jit(solution)/shard_map/while/body/eval_jaxpr/convert_element_type | solution.py:34
  165.1 0.9 multiply_reduce_fusion.3
  166.8 16.1 %multiply_convert_fusion.5 = (bf16[2,1024,512]{2,1,0:T(8,128)(2,1)S(1)}, bf16[2,1024,512]{2,1,0:T(8,128)(2,1)S(1)}) fusion(f32[1024,512]{1,0:T(8,128)S(1)} %get-tuple-element.158, f32[2]{0:T(128)S(1)} %bitcast.94, f32[1024,512]{1,0:T(8,128)S(1)} %get-tuple-element.159), kind=kLoop, calls=%fused_computation.2.clone.1 | loop fusion | flops 6291456 | bytes 8388616 | tf_op jit(solution)/shard_map/while/body/eval_jaxpr/convert_element_type | solution.py:34
  185.3 0.9 multiply_reduce_fusion.3
  186.9 16.1 %multiply_convert_fusion.5 = (bf16[2,1024,512]{2,1,0:T(8,128)(2,1)S(1)}, bf16[2,1024,512]{2,1,0:T(8,128)(2,1)S(1)}) fusion(f32[1024,512]{1,0:T(8,128)S(1)} %get-tuple-element.158, f32[2]{0:T(128)S(1)} %bitcast.94, f32[1024,512]{1,0:T(8,128)S(1)} %get-tuple-element.159), kind=kLoop, calls=%fused_computation.2.clone.1 | loop fusion | flops 6291456 | bytes 8388616 | tf_op jit(solution)/shard_map/while/body/eval_jaxpr/convert_element_type | solution.py:34
  205.4 0.9 multiply_reduce_fusion.3
  207.0 16.1 %multiply_convert_fusion.5 = (bf16[2,1024,512]{2,1,0:T(8,128)(2,1)S(1)}, bf16[2,1024,512]{2,1,0:T(8,128)(2,1)S(1)}) fusion(f32[1024,512]{1,0:T(8,128)S(1)} %get-tuple-element.158, f32[2]{0:T(128)S(1)} %bitcast.94, f32[1024,512]{1,0:T(8,128)S(1)} %get-tuple-element.159), kind=kLoop, calls=%fused_computation.2.clone.1 | loop fusion | flops 6291456 | bytes 8388616 | tf_op jit(solution)/shard_map/while/body/eval_jaxpr/convert_element_type | solution.py:34
  224.9 0.8 squeeze_reshape.3
  225.7 88.8 %all-reduce.2.cloned.1.call-done = f32[2,2,8192]{2,1,0:T(2,128)} async-done(((f32[2,2,8192]{2,1,0:T(2,128)}), f32[2,2,8192]{2,1,0:T(2,128)}) %all-reduce.2.cloned.1.call-update) | async-done | bytes 131088 | tf_op jit(solution)/shard_map/psum | solution.py:84
  315.2 134.6 %psum.15 = f32[1024]{0:T(1024)S(1)} all-reduce(f32[1024]{0:T(1024)S(1)} %multiply_reduce_fusion.1), channel_id=1, replica_groups=mesh['tm'=64,'mic'=8] {'tm'}, use_global_device_ids=true, to_apply=%region_5.6 | all-reduce | flops 1024 | bytes 8192 | tf_op jit(solution)/shard_map/psum | solution.py:87
  (93 shorter events, 26.3 us)
Async XLA Ops:
  6.5 307.9 %all-reduce.2.cloned.1.call-start = ((), (), s32[]{:S(2)}) async-start(), calls=%async_computation | async-start | bytes 262144 | tf_op jit(solution)/shard_map/psum | solution.py:84
  6.5 52.5 %collective-permute-start = (bf16[4096,512]{1,0:T(8,128)(2,1)}, bf16[4096,512]{1,0:T(8,128)(2,1)}, u32[]{:S(2)}, u32[]{:S(2)}) collective-permute-start(bf16[4096,512]{1,0:T(8,128)(2,1)} %param.6), channel_id=1, source_target_pairs={{8,0},{16,8},{24,16},{32,24},{40,32},{48,40},{56,48},{64,56},{72,6... | collective-permute-start | bytes 12582920 | tf_op jit(solution)/shard_map/ppermute | solution.py:16
  18.3 45.5 %copy-start = (s32[3,512]{1,0:T(4,128)S(1)}, s32[3,512]{1,0:T(4,128)}, u32[]{:S(2)}) copy-start(s32[3,512]{1,0:T(4,128)} %param.7) | copy-start | bytes 18436
Sparse Core Ops, SparseCore 0:
  225.8 88.5 all-reduce.1
where the time goes:
time: 458 us; the launch traced here: 457 us
  other arithmetic  147 us (32%)
  blocking collectives  135 us (29%)
  waiting for transfers between devices  130 us (28%)
  matrix products  16.7 us (4%)
  between operations  13.5 us (3%)
  starting transfers between devices  8.78 us (2%)
  local copies, waits for them, and re-layouts  6.75 us (1%)
    psum x1, blocking collectives, local(): power_sum = lax.psum(local_power, 'tm')  135 us
    convert_element_type x8, other arithmetic, steer_block(): (strength[None] * jnp.cos(2.0 * math.pi * cycles)).astype(jnp.bfloat16)  129 us
    psum x1, waiting for transfers between devices, local(): summed = lax.psum(partial_value, 'mic')  88.8 us
    ppermute x1, waiting for transfers between devices, from_behind(): return lax.ppermute(shard, axis, pairs)  40.8 us
  transfers between devices with their start and end apart: 2, of which 2 were waited for; matrix products, arithmetic and copies ran while one was open for 1% of the time, Pallas kernels for 0%

commit v1 on v0

v1 whole, which is shorter than its diff:
```python
import math

import jax
import jax.numpy as jnp
from jax import lax
from jax.experimental import pallas as pl
from jax.experimental.pallas import tpu as pltpu
from jax.sharding import PartitionSpec as P

MESH = pl.DeviceIdType.MESH
F32 = jnp.float32
BF16 = jnp.bfloat16

MICS = 4096
SEGLEN = 8192
NBINS = 2
SPAN = 4096
LOCAL_MICS = 512
DEPTHS = 16
PLANE = 4
OWNERS = 8
SHARE = 64
POINTS = OWNERS * SHARE
CHUNKS = 8
CHUNK = SPAN // CHUNKS
TILE = 16
EARLY = 16

SINE = (0.7071043846242844, -0.029459528423390287, 0.00036709000983827487, -2.0288338894692693e-06)
SINE_FINE = (
    0.707106764602781,
    -0.029462748844770903,
    0.0003682655953189757,
    -2.1877062853298923e-06,
    7.155046293945055e-09,
)
COSINE = (
    1.414213496370263,
    -0.17677635985529122,
    0.0036825749254888974,
    -3.061255945642025e-05,
    1.2790331792070752e-07,
)
TURN = 2.0 * math.pi
TURN_HIGH = 6.28125
TURN_LOW = TURN - TURN_HIGH
ROUNDER = 1.5 * 2.0**23


def poly(coefficients, x):
    value = coefficients[-1] * x + coefficients[-2]
    for c in coefficients[-3::-1]:
        value = value * x + c
    return value


def half_sine(f):
    return f * poly(SINE_FINE, f * f)


def table_chunk(index, bin_a, bin_b):
    row = lax.broadcasted_iota(jnp.int32, (8, CHUNK), 0)
    lane = lax.broadcasted_iota(jnp.int32, (8, CHUNK), 1)
    k = jnp.where((row & 2) == 0, bin_a, bin_b)
    sample = lane + index * CHUNK + (row >> 2) * SPAN
    phase = (k * sample + (row & 1) * (SEGLEN // 4)) & (SEGLEN - 1)
    s = half_sine((phase - SEGLEN // 2).astype(F32) * (TURN / SEGLEN))
    near = jnp.minimum(sample, SEGLEN - sample).astype(F32)
    w = half_sine(near * (TURN / SEGLEN))
    weighting = (0.5 / math.sqrt(0.375 * SEGLEN)) * (w * w)
    return (weighting * (s * s - 1.0)).astype(BF16)


def kernel(
    sig_hbm,
    mic_hbm,
    grid_hbm,
    bins_hbm,
    out_ref,
    sig,
    mic,
    grid,
    bins,
    mic_columns,
    grid_rows,
    own_half,
    next_half,
    halo,
    gathered,
    wide,
    x_ref,
    w_ref,
    part,
    arrived,
    plane,
    final,
    sig_sem,
    small_sem,
    halo_sem,
    gather_send,
    gather_recv,
    sum_send,
    sum_recv,
    plane_send,
    plane_recv,
    final_send,
    final_recv,
):
    t, j = lax.axis_index("tm"), lax.axis_index("mic")
    z, p = t // PLANE, t % PLANE
    spans = DEPTHS * PLANE
    before, after = lax.rem(t + spans - 1, spans), lax.rem(t + 1, spans)

    def depth(d):
        return lax.rem(z + d, DEPTHS) * PLANE + p

    def in_plane(d):
        return z * PLANE + lax.rem(p + d, PLANE)

    def owner(d):
        return lax.rem(j + d, OWNERS)

    small = [
        pltpu.make_async_copy(bins_hbm, bins, small_sem.at[0]),
        pltpu.make_async_copy(mic_hbm, mic, small_sem.at[1]),
        pltpu.make_async_copy(grid_hbm, grid, small_sem.at[2]),
    ]
    for copy in small:
        copy.start()
    loads = []
    for c in range(CHUNKS):
        rows = pl.ds(c * CHUNK, CHUNK)
        loads.append(pltpu.make_async_copy(sig_hbm.at[rows], sig.at[rows], sig_sem.at[c]))
        loads[-1].start()

    barrier = pltpu.get_barrier_semaphore()
    peers = [(before, j), (after, j)]
    peers += [(depth(d), j) for d in range(1, DEPTHS)]
    peers += [(in_plane(d), j) for d in range(1, PLANE)]
    peers += [(t, owner(d)) for d in range(1, OWNERS)]
    for peer in peers:
        pl.semaphore_signal(barrier, inc=1, device_id=peer, device_id_type=MESH)

    small[0].wait()
    bin_a, bin_b = bins[0], bins[1]
    tables = [table_chunk(c, bin_a, bin_b) for c in range(CHUNKS)]

    small[1].wait()
    small[2].wait()
    padded = jnp.concatenate([mic[...].astype(F32), jnp.zeros((5, LOCAL_MICS), F32)], axis=0)
    mic_columns[...] = padded.T
    odd = lax.rem(z, 2) == 1
    low_lanes = lax.broadcasted_iota(jnp.int32, (8, 128), 1) < SHARE
    window = (z // 2) * 128
    for coordinate in range(3):
        for a in range(OWNERS // 2):
            halves = []
            for side in range(2):
                start = pl.multiple_of((2 * a + side) * OWNERS * 128 + window, 128)
                row = grid[coordinate : coordinate + 1, pl.ds(start, 128)].astype(F32)
                row = jnp.broadcast_to(row, (8, 128))
                other = pltpu.roll(row, SHARE, 1)
                halves.append(jnp.where(odd, other, row) if side == 0 else jnp.where(odd, row, other))
            grid_rows[coordinate, :, a * 128 : (a + 1) * 128] = jnp.where(low_lanes, halves[0], halves[1])

    total = jnp.zeros((8, LOCAL_MICS), F32)
    for c in range(CHUNKS):
        loads[c].wait()
        total += jnp.dot(tables[c], sig[c * CHUNK : (c + 1) * CHUNK, :], preferred_element_type=F32)
    for c in range(4):
        block = total[:, c * 128 : (c + 1) * 128]
        own_half[4 * c : 4 * c + 4, :] = block[0:4]
        next_half[4 * c : 4 * c + 4, :] = block[4:8]

    pl.semaphore_wait(barrier, len(peers))
    halo_copy = pltpu.make_async_remote_copy(
        src_ref=next_half,
        dst_ref=halo,
        send_sem=halo_sem.at[0],
        recv_sem=halo_sem.at[1],
        device_id=(before, j),
        device_id_type=MESH,
    )
    halo_copy.start()

    bin_values = (bin_a.astype(F32), bin_b.astype(F32))

    def steer(step, carry):
        rows = pl.ds(pl.multiple_of(step * TILE, TILE), TILE)
        square = None
        for coordinate in range(3):
            column = mic_columns[rows, coordinate : coordinate + 1]
            points = grid_rows[coordinate, 0:1, :]
            offset = points - column
            square = offset * offset if square is None else square + offset * offset
        inverse = lax.rsqrt(square)
        distance = square * inverse
        strength = 16.0 * inverse
        for b in range(NBINS):
            angle = (bin_values[b] * distance) * (TURN / 512.0)
            turns = (angle * (1.0 / TURN) + ROUNDER) - ROUNDER
            f = (angle - turns * TURN_HIGH) - turns * TURN_LOW
            f2 = f * f
            s = f * poly(SINE, f2)
            c = poly(COSINE, f2)
            scaled = strength * s
            sine_rows = pl.ds(pl.multiple_of(step * TILE + LOCAL_MICS, TILE), TILE)
            w_ref[b, rows, :] = (strength - scaled * s).astype(BF16)
            w_ref[b, sine_rows, :] = (scaled * c).astype(BF16)
        return carry

    lax.fori_loop(0, EARLY, steer, 0)

    halo_copy.wait_recv()
    following = jnp.where(t == spans - 1, 0.0, halo[...])
    gathered[z] = (own_half[...] + following).astype(BF16)
    gather_copies = []
    for d in sorted(range(1, DEPTHS), key=lambda d: -min(d, DEPTHS - d)):
        copy = pltpu.make_async_remote_copy(
            src_ref=gathered.at[z],
            dst_ref=gathered.at[z],
            send_sem=gather_send.at[d],
            recv_sem=gather_recv.at[d],
            device_id=(depth(d), j),
            device_id_type=MESH,
        )
        copy.start()
        gather_copies.append((d, copy))

    lax.fori_loop(EARLY, LOCAL_MICS // TILE, steer, 0)

    for d in range(1, DEPTHS):
        slot = gathered.at[lax.rem(z + DEPTHS - d, DEPTHS)]
        pltpu.make_async_remote_copy(
            src_ref=slot,
            dst_ref=slot,
            send_sem=gather_send.at[d],
            recv_sem=gather_recv.at[d],
            device_id=(depth(d), j),
            device_id_type=MESH,
        ).wait_recv()

    for s in range(DEPTHS):
        wide[16 * s : 16 * s + 16, :] = gathered[s].astype(F32)
    for c in range(4):
        for b in range(NBINS):
            real = wide[pl.ds(4 * c + 2 * b, DEPTHS, stride=16), :]
            imag = wide[pl.ds(4 * c + 2 * b + 1, DEPTHS, stride=16), :]
            lanes = slice(128 * c, 128 * c + 128)
            sine_lanes = slice(LOCAL_MICS + 128 * c, LOCAL_MICS + 128 * c + 128)
            x_ref[b, 0:16, lanes] = real.astype(BF16)
            x_ref[b, 16:32, lanes] = imag.astype(BF16)
            x_ref[b, 0:16, sine_lanes] = (-imag).astype(BF16)
            x_ref[b, 16:32, sine_lanes] = real.astype(BF16)

    beams = [jnp.dot(x_ref[b], w_ref[b], preferred_element_type=F32) for b in range(NBINS)]
    low = lax.broadcasted_iota(jnp.int32, (32, 128), 1) < SHARE
    for a in range(OWNERS // 2):
        first, second = (beam[:, a * 128 : (a + 1) * 128] for beam in beams)
        part[2 * a] = jnp.where(low, first, pltpu.roll(second, SHARE, 1))
        part[2 * a + 1] = jnp.where(low, pltpu.roll(first, SHARE, 1), second)

    sum_copies = []
    for d in (4, 5, 3, 6, 2, 7, 1):
        copy = pltpu.make_async_remote_copy(
            src_ref=part.at[owner(d)],
            dst_ref=arrived.at[j],
            send_sem=sum_send.at[d],
            recv_sem=sum_recv.at[d],
            device_id=(t, owner(d)),
            device_id_type=MESH,
        )
        copy.start()
        sum_copies.append(copy)
    beam = part[j]
    for d in range(1, OWNERS):
        source = lax.rem(j + OWNERS - d, OWNERS)
        pltpu.make_async_remote_copy(
            src_ref=part.at[source],
            dst_ref=arrived.at[source],
            send_sem=sum_send.at[d],
            recv_sem=sum_recv.at[d],
            device_id=(t, owner(d)),
            device_id_type=MESH,
        ).wait_recv()
        beam += arrived[source]
    squares = beam * beam
    folded = squares[0:8] + squares[8:16] + squares[16:24] + squares[24:32]
    folded += pltpu.roll(folded, SHARE, 1)
    plane[p] = jnp.sum(folded, axis=0, keepdims=True)

    plane_copies = []
    for d in range(1, PLANE):
        copy = pltpu.make_async_remote_copy(
            src_ref=plane.at[p],
            dst_ref=plane.at[p],
            send_sem=plane_send.at[d],
            recv_sem=plane_recv.at[d],
            device_id=(in_plane(d), j),
            device_id_type=MESH,
        )
        copy.start()
        plane_copies.append(copy)
    for d in range(1, PLANE):
        slot = plane.at[lax.rem(p + PLANE - d, PLANE)]
        pltpu.make_async_remote_copy(
            src_ref=slot,
            dst_ref=slot,
            send_sem=plane_send.at[d],
            recv_sem=plane_recv.at[d],
            device_id=(in_plane(d), j),
            device_id_type=MESH,
        ).wait_recv()
    final[z] = (plane[0] + plane[1]) + (plane[2] + plane[3])

    final_copies = []
    for d in sorted(range(1, DEPTHS), key=lambda d: -min(d, DEPTHS - d)):
        copy = pltpu.make_async_remote_copy(
            src_ref=final.at[z],
            dst_ref=final.at[z],
            send_sem=final_send.at[d],
            recv_sem=final_recv.at[d],
            device_id=(depth(d), j),
            device_id_type=MESH,
        )
        copy.start()
        final_copies.append(copy)
    halo_copy.wait_send()
    for _, copy in gather_copies:
        copy.wait_send()
    for copy in sum_copies + plane_copies + final_copies:
        copy.wait_send()
    for d in range(1, DEPTHS):
        slot = final.at[lax.rem(z + DEPTHS - d, DEPTHS)]
        pltpu.make_async_remote_copy(
            src_ref=slot,
            dst_ref=slot,
            send_sem=final_send.at[d],
            recv_sem=final_recv.at[d],
            device_id=(depth(d), j),
            device_id_type=MESH,
        ).wait_recv()
    first_lanes = lax.broadcasted_iota(jnp.int32, (1, 128), 1) < SHARE
    scale = 1.0 / (spans * NBINS * MICS)
    for r in range(DEPTHS // 2):
        out_ref[r : r + 1, :] = jnp.where(first_lanes, final[2 * r], final[2 * r + 1]) * scale


def local(signal, mic_pos, grid_pos, bins):
    hbm = pl.BlockSpec(memory_space=pl.ANY)
    dma = pltpu.SemaphoreType.DMA
    power = pl.pallas_call(
        kernel,
        out_shape=jax.ShapeDtypeStruct((DEPTHS // 2, 128), F32),
        in_specs=[hbm] * 4,
        out_specs=pl.BlockSpec(memory_space=pltpu.VMEM),
        scratch_shapes=[
            pltpu.VMEM((SPAN, LOCAL_MICS), BF16),
            pltpu.VMEM(mic_pos.shape, jnp.int32),
            pltpu.VMEM(grid_pos.shape, jnp.int32),
            pltpu.SMEM(bins.shape, jnp.int32),
            pltpu.VMEM((LOCAL_MICS, 8), F32),
            pltpu.VMEM((3, 8, POINTS), F32),
            pltpu.VMEM((16, 128), F32),
            pltpu.VMEM((16, 128), F32),
            pltpu.VMEM((16, 128), F32),
            pltpu.VMEM((DEPTHS, 16, 128), BF16),
            pltpu.VMEM((DEPTHS * 16, 128), F32),
            pltpu.VMEM((NBINS, 2 * DEPTHS, 2 * LOCAL_MICS), BF16),
            pltpu.VMEM((NBINS, 2 * LOCAL_MICS, POINTS), BF16),
            pltpu.VMEM((OWNERS, 2 * DEPTHS, 128), F32),
            pltpu.VMEM((OWNERS, 2 * DEPTHS, 128), F32),
            pltpu.VMEM((PLANE, 1, 128), F32),
            pltpu.VMEM((DEPTHS, 1, 128), F32),
            dma((CHUNKS,)),
            dma((3,)),
            dma((2,)),
            dma((DEPTHS,)),
            dma((DEPTHS,)),
            dma((OWNERS,)),
            dma((OWNERS,)),
            dma((PLANE,)),
            dma((PLANE,)),
            dma((DEPTHS,)),
            dma((DEPTHS,)),
        ],
        compiler_params=pltpu.CompilerParams(
            collective_id=0, has_side_effects=True, vmem_limit_bytes=32 * 1024 * 1024
        ),
    )(signal, mic_pos, grid_pos, bins)
    return power.reshape(-1)


def solution(mesh):
    in_specs = (P("tm", "mic"), P(None, "mic"), P(), P())
    out_specs = P("mic")
    return jax.shard_map(local, mesh=mesh, in_specs=in_specs, out_specs=out_specs, check_vma=False)
```

time: 458 us -> 49.4 us (0.11)
  other arithmetic: 147 us -> 0 us
  blocking collectives: 135 us -> 0 us
  waiting for transfers between devices: 130 us -> 0 us
  Pallas kernels: 0 us -> 44.1 us
  matrix products: 16.7 us -> 0 us
  between operations: 13.5 us -> 0.01 us
  starting transfers between devices: 8.78 us -> 0 us
    psum x1 -> x0, blocking collectives: 135 us -> none  [local(): power_sum = lax.psum(local_power, 'tm')]
    convert_element_type x9 -> x0, other arithmetic: 130 us -> none  [the longest x8 129 us: steer_block(): (strength[None] * jnp.cos(2.0 * math.pi * cycles)).astype(jnp.bfloat16)]
    psum x1 -> x0, waiting for transfers between devices: 88.8 us -> none  [local(): summed = lax.psum(partial_value, 'mic')]
    pallas_call x0 -> x1, Pallas kernels: none -> 44.1 us  [local(): pl.pallas_call(kernel, out_shape=jax.ShapeDtypeStruct((DEPTHS // 2, 128),...]
    ppermute x1 -> x0, waiting for transfers between devices: 40.8 us -> none  [from_behind(): return lax.ppermute(shard, axis, pairs)]
    dot_general x33 -> x0, matrix products: 16.7 us -> none  [the longest x16 6.15 us: steered(): jnp.dot(bin_pair, cosine_part[bin_index].T, preferred_element_type=jnp.fl...]
    ppermute x1 -> x0, starting transfers between devices: 8.78 us -> none  [from_behind(): return lax.ppermute(shard, axis, pairs)]
    reduce_sum x9 -> x0, other arithmetic: 8.28 us -> none  [the longest x8 7.54 us: steer_block(): distance = jnp.sqrt(jnp.sum(offsets * offsets, axis=0).astype(jnp.float32))]
  transfers between devices with their start and end apart: 2 -> 0, of which waited for: 2 -> 0; matrix products, arithmetic and copies ran while one was open for 1% -> 0% of each run, Pallas kernels for 0% -> 0%
where the time goes in v1:
time: 49.4 us; the launch traced here: 49.2 us
  Pallas kernels  44.1 us (89%)
  local copies, waits for them, and re-layouts  5.04 us (10%)
    pallas_call x1, Pallas kernels, local(): pl.pallas_call(kernel, out_shape=jax.ShapeDtypeStruct((DEPTHS // 2, 128),...  44.1 us
    unnamed x9, local copies, waits for them, and re-layouts  5.04 us

profile of v1, /device:TPU:1, one launch (start us, length us, event | category | flops | bytes accessed | tf_op | source)
XLA Modules:
  0.0 49.2 jit_solution(9190725537064037101)
XLA Ops:
  0.0 0.0 copy-start
  0.0 2.2 %copy-done = bf16[4096,512]{1,0:T(8,128)(2,1)S(1)} copy-done((bf16[4096,512]{1,0:T(8,128)(2,1)S(1)}, bf16[4096,512]{1,0:T(8,128)(2,1)}, u32[]{:S(2)}) %copy-start) | copy-done | bytes 4194328
  2.2 0.0 copy-start.1
  2.2 0.9 %copy-done.1 = s32[3,8192]{1,0:T(4,128)S(1)} copy-done((s32[3,8192]{1,0:T(4,128)S(1)}, s32[3,8192]{1,0:T(4,128)}, u32[]{:S(2)}) %copy-start.1) | copy-done | bytes 98328
  3.1 0.0 copy-start.2
  3.1 0.7 %copy-done.2 = s32[3,512]{1,0:T(4,128)S(1)} copy-done((s32[3,512]{1,0:T(4,128)S(1)}, s32[3,512]{1,0:T(4,128)}, u32[]{:S(2)}) %copy-start.2) | copy-done | bytes 6168
  3.8 0.0 copy-start.3
  3.8 0.7 %copy-done.3 = s32[2]{0:T(128)S(1)} copy-done((s32[2]{0:T(128)S(1)}, s32[2]{0:T(128)}, u32[]{:S(2)}) %copy-start.3) | copy-done | bytes 32
  4.4 44.1 %shard_map.46 = f32[8,128]{1,0:T(8,128)S(1)} custom-call(bf16[4096,512]{1,0:T(8,128)(2,1)S(1)} %copy-done, s32[3,512]{1,0:T(4,128)S(1)} %copy-done.2, s32[3,8192]{1,0:T(4,128)S(1)} %copy-done.1, s32[2]{0:T(128)S(1)} %copy-done.3), custom_call_target="tpu_custom_call" | custom-call | tf_op jit(solution)/shard_map/pallas_call | solution.py:352
  48.6 0.6 %copy.6 = f32[1024]{0:T(1024)} copy(f32[1024]{0:T(1024)S(1)} %bitcast.1) | data formatting | bytes 8192
Async XLA Ops:
  0.0 2.2 %copy-start = (bf16[4096,512]{1,0:T(8,128)(2,1)S(1)}, bf16[4096,512]{1,0:T(8,128)(2,1)}, u32[]{:S(2)}) copy-start(bf16[4096,512]{1,0:T(8,128)(2,1)} %sig_hbm.1) | copy-start | bytes 12582916
  2.2 0.9 %copy-start.1 = (s32[3,8192]{1,0:T(4,128)S(1)}, s32[3,8192]{1,0:T(4,128)}, u32[]{:S(2)}) copy-start(s32[3,8192]{1,0:T(4,128)} %grid_hbm.1) | copy-start | bytes 294916
  3.1 0.7 %copy-start.2 = (s32[3,512]{1,0:T(4,128)S(1)}, s32[3,512]{1,0:T(4,128)}, u32[]{:S(2)}) copy-start(s32[3,512]{1,0:T(4,128)} %mic_hbm.1) | copy-start | bytes 18436
  3.8 0.7 %copy-start.3 = (s32[2]{0:T(128)S(1)}, s32[2]{0:T(128)}, u32[]{:S(2)}) copy-start(s32[2]{0:T(128)} %bins_hbm.1) | copy-start | bytes 28

commit v2 on v1

v2 whole, which is shorter than its diff:
```python
import math

import jax
import jax.numpy as jnp
from jax import lax
from jax.experimental import pallas as pl
from jax.experimental.pallas import tpu as pltpu
from jax.sharding import PartitionSpec as P

MESH = pl.DeviceIdType.MESH
F32 = jnp.float32
BF16 = jnp.bfloat16

MICS = 4096
SEGLEN = 8192
NBINS = 2
SPAN = 4096
LOCAL_MICS = 512
SPANS = 64
GROUP = 8
GROUPS = SPANS // GROUP
OWNERS = 8
SHARE = 128
POINTS = OWNERS * SHARE
CHUNKS = 8
CHUNK = SPAN // CHUNKS
TILE = 32
WIDTH = 512
TILES = LOCAL_MICS // TILE
STEPS = TILES * POINTS // WIDTH
EARLY = 4

SINE = (0.7071043846242844, -0.029459528423390287, 0.00036709000983827487, -2.0288338894692693e-06)
SINE_FINE = (
    0.707106764602781,
    -0.029462748844770903,
    0.0003682655953189757,
    -2.1877062853298923e-06,
    7.155046293945055e-09,
)
COSINE = (
    1.414213496370263,
    -0.17677635985529122,
    0.0036825749254888974,
    -3.061255945642025e-05,
    1.2790331792070752e-07,
)
TURN = 2.0 * math.pi
TURN_HIGH = 6.28125
TURN_LOW = TURN - TURN_HIGH
ROUNDER = 1.5 * 2.0**23


def poly(coefficients, x):
    value = coefficients[-1] * x + coefficients[-2]
    for c in coefficients[-3::-1]:
        value = value * x + c
    return value


def half_sine(f):
    return f * poly(SINE_FINE, f * f)


def table_chunk(index, bin_a, bin_b):
    row = lax.broadcasted_iota(jnp.int32, (8, CHUNK), 0)
    lane = lax.broadcasted_iota(jnp.int32, (8, CHUNK), 1)
    k = jnp.where((row & 2) == 0, bin_a, bin_b)
    sample = lane + index * CHUNK + (row >> 2) * SPAN
    phase = (k * sample + (row & 1) * (SEGLEN // 4)) & (SEGLEN - 1)
    s = half_sine((phase - SEGLEN // 2).astype(F32) * (TURN / SEGLEN))
    near = jnp.minimum(sample, SEGLEN - sample).astype(F32)
    w = half_sine(near * (TURN / SEGLEN))
    weighting = (0.5 / math.sqrt(0.375 * SEGLEN)) * (w * w)
    return (weighting * (s * s - 1.0)).astype(BF16)


def flip(index, bits, mask):
    value = 0
    for bit in range(bits):
        digit = (index // (1 << bit)) % 2
        value = value + (1 << bit) * (1 - digit if mask >> bit & 1 else digit)
    return value


def kernel(
    sig_hbm,
    mic_hbm,
    grid_hbm,
    bins_hbm,
    out_ref,
    sig,
    mic,
    grid,
    bins,
    mic_columns,
    grid_rows,
    halves,
    following,
    wide,
    x_ref,
    w_ref,
    part,
    arrived,
    final,
    sig_sem,
    small_sem,
    lead_send,
    lead_recv,
    group_send,
    group_recv,
    sum_send,
    sum_recv,
    final_send,
    final_recv,
    far_sem,
):
    t, j = lax.axis_index("tm"), lax.axis_index("mic")
    k, g = t // GROUP, t % GROUP

    def member(mask):
        return k * GROUP + flip(g, 3, mask)

    def column(d):
        return lax.rem(t + SPANS + d * GROUP, SPANS)

    small = [
        pltpu.make_async_copy(bins_hbm, bins, small_sem.at[0]),
        pltpu.make_async_copy(mic_hbm, mic, small_sem.at[1]),
        pltpu.make_async_copy(grid_hbm, grid, small_sem.at[2]),
    ]
    for copy in small:
        copy.start()
    loads = []
    for c in range(CHUNKS):
        rows = pl.ds(c * CHUNK, CHUNK)
        loads.append(pltpu.make_async_copy(sig_hbm.at[rows], sig.at[rows], sig_sem.at[c]))
        loads[-1].start()

    barrier = pltpu.get_barrier_semaphore()
    next_leader = lax.rem(k + 1, GROUPS) * GROUP
    near = [(column(d), j) for d in (-2, 2, -1, 1)]
    near += [(member(m), j) for m in (7, 6, 3, 2, 5, 4, 1)]
    near += [(t, lax.rem(j + d, OWNERS)) for d in range(1, OWNERS)]
    for peer in [(next_leader, j)] + near:
        pl.semaphore_signal(barrier, inc=1, device_id=peer, device_id_type=MESH)

    small[0].wait()
    bin_a, bin_b = bins[0], bins[1]
    tables = [table_chunk(c, bin_a, bin_b) for c in range(CHUNKS)]

    small[1].wait()
    small[2].wait()
    padded = jnp.concatenate([mic[...].astype(F32), jnp.zeros((5, LOCAL_MICS), F32)], axis=0)
    mic_columns[...] = padded.T
    for o in range(OWNERS):
        start = pl.multiple_of((o * GROUP + g) * SHARE, SHARE)
        for coordinate in range(3):
            row = grid[coordinate : coordinate + 1, pl.ds(start, SHARE)].astype(F32)
            grid_rows[coordinate : coordinate + 1, o * SHARE : (o + 1) * SHARE] = row

    bin_values = (bin_a.astype(F32), bin_b.astype(F32))

    def steer(step, carry):
        tile, side = step % TILES, step // TILES
        rows = pl.ds(pl.multiple_of(tile * TILE, TILE), TILE)
        sine_rows = pl.ds(pl.multiple_of(tile * TILE + LOCAL_MICS, TILE), TILE)
        lanes = pl.ds(pl.multiple_of(side * WIDTH, WIDTH), WIDTH)
        square = None
        for coordinate in range(3):
            column = mic_columns[rows, coordinate : coordinate + 1]
            offset = grid_rows[coordinate : coordinate + 1, lanes] - column
            square = offset * offset if square is None else square + offset * offset
        inverse = lax.rsqrt(square)
        distance = square * inverse
        strength = 16.0 * inverse
        for b in range(NBINS):
            angle = (bin_values[b] * distance) * (TURN / 512.0)
            turns = (angle * (1.0 / TURN) + ROUNDER) - ROUNDER
            f = (angle - turns * TURN_HIGH) - turns * TURN_LOW
            f2 = f * f
            s = f * poly(SINE, f2)
            c = poly(COSINE, f2)
            scaled = strength * s
            w_ref[b, rows, lanes] = (strength - scaled * s).astype(BF16)
            w_ref[b, sine_rows, lanes] = (scaled * c).astype(BF16)
        return carry

    lax.fori_loop(0, EARLY, steer, 0)

    total = jnp.zeros((8, LOCAL_MICS), F32)
    for c in range(CHUNKS):
        loads[c].wait()
        total += jnp.dot(tables[c], sig[c * CHUNK : (c + 1) * CHUNK, :], preferred_element_type=F32)
    for c in range(4):
        block = total[:, c * 128 : (c + 1) * 128]
        halves[g, 0, 4 * c : 4 * c + 4, :] = block[0:4]
        halves[g, 1, 4 * c : 4 * c + 4, :] = block[4:8]

    leader = g == 0
    pl.semaphore_wait(barrier, jnp.where(leader, len(near) + GROUP, len(near)))
    previous = lax.rem(k + GROUPS - 1, GROUPS) * GROUP
    lead_copies = [
        pltpu.make_async_remote_copy(
            src_ref=halves.at[0, 1],
            dst_ref=following,
            send_sem=lead_send.at[i],
            recv_sem=lead_recv,
            device_id=(previous + i, j),
            device_id_type=MESH,
        )
        for i in range(GROUP)
    ]

    @pl.when(leader)
    def _():
        for copy in lead_copies:
            copy.start()

    group_copies = []
    for m in (7, 6, 3, 2, 5, 4, 1):
        copy = pltpu.make_async_remote_copy(
            src_ref=halves.at[g],
            dst_ref=halves.at[g],
            send_sem=group_send.at[m],
            recv_sem=group_recv.at[m],
            device_id=(member(m), j),
            device_id_type=MESH,
        )
        copy.start()
        group_copies.append(copy)
    for d in (-2, 2):
        pl.semaphore_signal(far_sem.at[0], inc=1, device_id=(column(d), j), device_id_type=MESH)

    lax.fori_loop(EARLY, STEPS, steer, 0)

    pl.semaphore_wait(far_sem.at[0], 2)
    for m in range(1, GROUP):
        pl.semaphore_signal(far_sem.at[1], inc=1, device_id=(member(m), j), device_id_type=MESH)

    for m in (1, 4, 5, 2, 3, 6, 7):
        slot = halves.at[flip(g, 3, m)]
        pltpu.make_async_remote_copy(
            src_ref=slot,
            dst_ref=slot,
            send_sem=group_send.at[m],
            recv_sem=group_recv.at[m],
            device_id=(member(m), j),
            device_id_type=MESH,
        ).wait_recv()
    lead_copies[0].wait_recv()

    for s in range(GROUP):
        if s < GROUP - 1:
            second = halves[s + 1, 1]
        else:
            second = jnp.where(k == GROUPS - 1, 0.0, following[...])
        wide[16 * s : 16 * s + 16, :] = halves[s, 0] + second
    for c in range(4):
        for b in range(NBINS):
            real = wide[pl.ds(4 * c + 2 * b, GROUP, stride=16), :]
            imag = wide[pl.ds(4 * c + 2 * b + 1, GROUP, stride=16), :]
            lanes = slice(128 * c, 128 * c + 128)
            sine_lanes = slice(LOCAL_MICS + 128 * c, LOCAL_MICS + 128 * c + 128)
            x_ref[b, :, lanes] = jnp.concatenate([real, imag], axis=0).astype(BF16)
            x_ref[b, :, sine_lanes] = jnp.concatenate([-imag, real], axis=0).astype(BF16)

    def start_sum(destination):
        copy = pltpu.make_async_remote_copy(
            src_ref=part.at[destination],
            dst_ref=arrived.at[j],
            send_sem=sum_send.at[destination],
            recv_sem=sum_recv.at[j],
            device_id=(t, destination),
            device_id_type=MESH,
        )
        copy.start()
        return copy

    sum_copies = []
    for mask in (3, 1, 2, 0):
        pair = flip(j // 2, 2, mask)
        lanes = pl.ds(pl.multiple_of(pair * 2 * SHARE, 2 * SHARE), 2 * SHARE)
        for b in range(NBINS):
            beam = jnp.dot(x_ref[b], w_ref[b, :, lanes], preferred_element_type=F32)
            part[2 * pair, 16 * b : 16 * b + 16, :] = beam[:, :SHARE]
            part[2 * pair + 1, 16 * b : 16 * b + 16, :] = beam[:, SHARE:]
        if mask:
            sum_copies += [start_sum(2 * pair), start_sum(2 * pair + 1)]
        else:
            sum_copies.append(start_sum(2 * pair + 1 - j % 2))
    beam = part[j]
    for d in range(1, OWNERS):
        source = lax.rem(j + OWNERS - d, OWNERS)
        pltpu.make_async_remote_copy(
            src_ref=part.at[source],
            dst_ref=arrived.at[source],
            send_sem=sum_send.at[source],
            recv_sem=sum_recv.at[source],
            device_id=(t, source),
            device_id_type=MESH,
        ).wait_recv()
        beam += arrived[source]
    squares = beam * beam
    folded = squares[0:8] + squares[8:16] + squares[16:24] + squares[24:32]
    final[t] = jnp.sum(folded, axis=0, keepdims=True)

    pl.semaphore_wait(far_sem.at[1], GROUP - 1)
    for d in sorted(range(1, SPANS), key=lambda d: -min(d, SPANS - d)):
        pltpu.make_async_remote_copy(
            src_ref=final.at[t],
            dst_ref=final.at[t],
            send_sem=final_send,
            recv_sem=final_recv,
            device_id=(lax.rem(t + d, SPANS), j),
            device_id_type=MESH,
        ).start()

    @pl.when(leader)
    def _():
        for copy in lead_copies:
            copy.wait_send()

    for copy in group_copies + sum_copies:
        copy.wait_send()
    others = final.at[pl.ds(0, SPANS - 1)]
    rest = pltpu.make_async_remote_copy(
        src_ref=others,
        dst_ref=others,
        send_sem=final_send,
        recv_sem=final_recv,
        device_id=(column(1), j),
        device_id_type=MESH,
    )
    rest.wait_send()
    rest.wait_recv()
    scale = 1.0 / (SPANS * NBINS * MICS)
    for i in range(GROUP):
        row = final[i]
        for n in range(1, GROUPS):
            row += final[GROUP * n + i]
        out_ref[i : i + 1, :] = row * scale


def local(signal, mic_pos, grid_pos, bins):
    dma = pltpu.SemaphoreType.DMA
    operands = [pltpu.with_memory_space_constraint(a, pltpu.HBM) for a in (signal, mic_pos, grid_pos, bins)]
    power = pl.pallas_call(
        kernel,
        out_shape=pltpu.VMEM((GROUP, SHARE), F32),
        in_specs=[pl.BlockSpec(memory_space=pl.ANY)] * 4,
        out_specs=pl.BlockSpec(memory_space=pltpu.VMEM),
        scratch_shapes=[
            pltpu.VMEM((SPAN, LOCAL_MICS), BF16),
            pltpu.VMEM(mic_pos.shape, jnp.int32),
            pltpu.VMEM(grid_pos.shape, jnp.int32),
            pltpu.SMEM(bins.shape, jnp.int32),
            pltpu.VMEM((LOCAL_MICS, 8), F32),
            pltpu.VMEM((8, POINTS), F32),
            pltpu.VMEM((GROUP, 2, 16, 128), F32),
            pltpu.VMEM((16, 128), F32),
            pltpu.VMEM((GROUP * 16, 128), F32),
            pltpu.VMEM((NBINS, 2 * GROUP, 2 * LOCAL_MICS), BF16),
            pltpu.VMEM((NBINS, 2 * LOCAL_MICS, POINTS), BF16),
            pltpu.VMEM((OWNERS, 4 * GROUP, SHARE), F32),
            pltpu.VMEM((OWNERS, 4 * GROUP, SHARE), F32),
            pltpu.VMEM((SPANS, 1, SHARE), F32),
            dma((CHUNKS,)),
            dma((3,)),
            dma((GROUP,)),
            dma,
            dma((GROUP,)),
            dma((GROUP,)),
            dma((OWNERS,)),
            dma((OWNERS,)),
            dma,
            dma,
            pltpu.SemaphoreType.REGULAR((2,)),
        ],
        compiler_params=pltpu.CompilerParams(
            collective_id=0, has_side_effects=True, vmem_limit_bytes=32 * 1024 * 1024
        ),
    )(*operands)
    return power.reshape(-1)


def solution(mesh):
    in_specs = (P("tm", "mic"), P(None, "mic"), P(), P())
    out_specs = P("mic")
    return jax.shard_map(local, mesh=mesh, in_specs=in_specs, out_specs=out_specs, check_vma=False)
```

time: 49.4 us -> 37.1 us (0.75)
  Pallas kernels: 44.1 us -> 36.4 us
  local copies, waits for them, and re-layouts: 5.04 us -> 0.6 us
    pallas_call x1, Pallas kernels: 44.1 us -> 36.4 us  [local(): pl.pallas_call(kernel, out_shape=pltpu.VMEM((GROUP, SHARE), F32), in_spec...]
    unnamed x9 -> x1, local copies, waits for them, and re-layouts: 5.04 us -> 0.6 us
where the time goes in v2:
time: 37.1 us; the launch traced here: 37 us
  Pallas kernels  36.4 us (98%)
  local copies, waits for them, and re-layouts  0.6 us (2%)
    pallas_call x1, Pallas kernels, local(): pl.pallas_call(kernel, out_shape=pltpu.VMEM((GROUP, SHARE), F32), in_spec...  36.4 us

profile of v2, /device:TPU:1, one launch (start us, length us, event | category | flops | bytes accessed | tf_op | source)
XLA Modules:
  0.0 37.0 jit_solution(16727719101777355455)
XLA Ops:
  0.0 36.4 %shard_map.46 = f32[8,128]{1,0:T(8,128)S(1)} custom-call(bf16[4096,512]{1,0:T(8,128)(2,1)} %sig_hbm.1, s32[3,512]{1,0:T(4,128)} %mic_hbm.1, s32[3,8192]{1,0:T(4,128)} %grid_hbm.1, s32[2]{0:T(128)} %bins_hbm.1), custom_call_target="tpu_custom_call" | custom-call | tf_op jit(solution)/shard_map/pallas_call | solution.py:348
  36.4 0.6 %copy.6 = f32[1024]{0:T(1024)} copy(f32[1024]{0:T(1024)S(1)} %bitcast.1) | data formatting | bytes 8192

commit v3 on v2

--- a/solution.py
+++ b/solution.py
@@ -24,13 +24,15 @@
 POINTS = OWNERS * SHARE
 CHUNKS = 8
 CHUNK = SPAN // CHUNKS
-TILE = 32
-WIDTH = 512
+TILE = 64
+PAIR = 2 * SHARE
 TILES = LOCAL_MICS // TILE
-STEPS = TILES * POINTS // WIDTH
-EARLY = 4
-
-SINE = (0.7071043846242844, -0.029459528423390287, 0.00036709000983827487, -2.0288338894692693e-06)
+STEPS = TILES * OWNERS // 2
+PORTIONS = ((0, 6), (6, 8))
+
+UNIT = 544.5
+SINE = (-0.020778089505148072, 0.22160904131003262, -0.7069151550432146, 1.0)
+COSINE = (0.0025972698674584724, -0.08311238928243203, 0.4432205811375266, -0.9426014873154713, 1.0)
 SINE_FINE = (
     0.707106764602781,
     -0.029462748844770903,
@@ -38,13 +40,6 @@
     -2.1877062853298923e-06,
     7.155046293945055e-09,
 )
-COSINE = (
-    1.414213496370263,
-    -0.17677635985529122,
-    0.0036825749254888974,
-    -3.061255945642025e-05,
-    1.2790331792070752e-07,
-)
 TURN = 2.0 * math.pi
 TURN_HIGH = 6.28125
 TURN_LOW = TURN - TURN_HIGH
@@ -52,7 +47,8 @@
 
 
 def poly(coefficients, x):
-    value = coefficients[-1] * x + coefficients[-2]
+    value = x if coefficients[-1] == 1.0 else coefficients[-1] * x
+    value = value + coefficients[-2]
     for c in coefficients[-3::-1]:
         value = value * x + c
     return value
@@ -121,6 +117,10 @@
     def member(mask):
         return k * GROUP + flip(g, 3, mask)
 
+    def owner(place):
+        across, along = ((1, 2), (1, 1), (1, 3), (0, 2), (1, 0), (0, 1), (0, 3), (0, 0))[place]
+        return flip(j // 4, 1, across) * 4 + lax.rem(j + along, 4)
+
     def column(d):
         return lax.rem(t + SPANS + d * GROUP, SPANS)
 
@@ -154,7 +154,7 @@
     padded = jnp.concatenate([mic[...].astype(F32), jnp.zeros((5, LOCAL_MICS), F32)], axis=0)
     mic_columns[...] = padded.T
     for o in range(OWNERS):
-        start = pl.multiple_of((o * GROUP + g) * SHARE, SHARE)
+        start = pl.multiple_of((owner(o) * GROUP + g) * SHARE, SHARE)
         for coordinate in range(3):
             row = grid[coordinate : coordinate + 1, pl.ds(start, SHARE)].astype(F32)
             grid_rows[coordinate : coordinate + 1, o * SHARE : (o + 1) * SHARE] = row
@@ -162,10 +162,10 @@
     bin_values = (bin_a.astype(F32), bin_b.astype(F32))
 
     def steer(step, carry):
-        tile, side = step % TILES, step // TILES
+        tile, pair = step % TILES, step // TILES
         rows = pl.ds(pl.multiple_of(tile * TILE, TILE), TILE)
         sine_rows = pl.ds(pl.multiple_of(tile * TILE + LOCAL_MICS, TILE), TILE)
-        lanes = pl.ds(pl.multiple_of(side * WIDTH, WIDTH), WIDTH)
+        lanes = pl.ds(pl.multiple_of(pair * PAIR, PAIR), PAIR)
         square = None
         for coordinate in range(3):
             column = mic_columns[rows, coordinate : coordinate + 1]
@@ -174,24 +174,24 @@
         inverse = lax.rsqrt(square)
         distance = square * inverse
         strength = 16.0 * inverse
+        weight = (16.0 * UNIT * UNIT) * inverse
         for b in range(NBINS):
-            angle = (bin_values[b] * distance) * (TURN / 512.0)
-            turns = (angle * (1.0 / TURN) + ROUNDER) - ROUNDER
-            f = (angle - turns * TURN_HIGH) - turns * TURN_LOW
-            f2 = f * f
-            s = f * poly(SINE, f2)
-            c = poly(COSINE, f2)
-            scaled = strength * s
+            angle = (bin_values[b] * distance) * (-TURN / 8192.0)
+            turns = (angle * (16.0 / TURN) + ROUNDER) - ROUNDER
+            h = (angle - turns * (TURN_HIGH / 16.0)) - turns * (TURN_LOW / 16.0)
+            h2 = h * h
+            s = h * poly(SINE, h2)
+            c = poly(COSINE, h2)
+            scaled = weight * s
             w_ref[b, rows, lanes] = (strength - scaled * s).astype(BF16)
             w_ref[b, sine_rows, lanes] = (scaled * c).astype(BF16)
         return carry
-
-    lax.fori_loop(0, EARLY, steer, 0)
 
     total = jnp.zeros((8, LOCAL_MICS), F32)
     for c in range(CHUNKS):
         loads[c].wait()
         total += jnp.dot(tables[c], sig[c * CHUNK : (c + 1) * CHUNK, :], preferred_element_type=F32)
+        steer(c, 0)
     for c in range(4):
         block = total[:, c * 128 : (c + 1) * 128]
         halves[g, 0, 4 * c : 4 * c + 4, :] = block[0:4]
@@ -232,7 +232,8 @@
     for d in (-2, 2):
         pl.semaphore_signal(far_sem.at[0], inc=1, device_id=(column(d), j), device_id_type=MESH)
 
-    lax.fori_loop(EARLY, STEPS, steer, 0)
+    ready = PORTIONS[0][1] // 2 * TILES
+    lax.fori_loop(CHUNKS, ready, steer, 0)
 
     pl.semaphore_wait(far_sem.at[0], 2)
     for m in range(1, GROUP):
@@ -265,42 +266,30 @@
             x_ref[b, :, lanes] = jnp.concatenate([real, imag], axis=0).astype(BF16)
             x_ref[b, :, sine_lanes] = jnp.concatenate([-imag, real], axis=0).astype(BF16)
 
-    def start_sum(destination):
-        copy = pltpu.make_async_remote_copy(
-            src_ref=part.at[destination],
-            dst_ref=arrived.at[j],
-            send_sem=sum_send.at[destination],
-            recv_sem=sum_recv.at[j],
-            device_id=(t, destination),
-            device_id_type=MESH,
-        )
-        copy.start()
-        return copy
-
     sum_copies = []
-    for mask in (3, 1, 2, 0):
-        pair = flip(j // 2, 2, mask)
-        lanes = pl.ds(pl.multiple_of(pair * 2 * SHARE, 2 * SHARE), 2 * SHARE)
+    for first, end in PORTIONS:
+        if first:
+            lax.fori_loop(first // 2 * TILES, end // 2 * TILES, steer, 0)
+        lanes = slice(first * SHARE, end * SHARE)
         for b in range(NBINS):
             beam = jnp.dot(x_ref[b], w_ref[b, :, lanes], preferred_element_type=F32)
-            part[2 * pair, 16 * b : 16 * b + 16, :] = beam[:, :SHARE]
-            part[2 * pair + 1, 16 * b : 16 * b + 16, :] = beam[:, SHARE:]
-        if mask:
-            sum_copies += [start_sum(2 * pair), start_sum(2 * pair + 1)]
-        else:
-            sum_copies.append(start_sum(2 * pair + 1 - j % 2))
-    beam = part[j]
-    for d in range(1, OWNERS):
-        source = lax.rem(j + OWNERS - d, OWNERS)
-        pltpu.make_async_remote_copy(
-            src_ref=part.at[source],
-            dst_ref=arrived.at[source],
-            send_sem=sum_send.at[source],
-            recv_sem=sum_recv.at[source],
-            device_id=(t, source),
-            device_id_type=MESH,
-        ).wait_recv()
-        beam += arrived[source]
+            for o in range(end - first):
+                part[first + o, 16 * b : 16 * b + 16, :] = beam[:, o * SHARE : (o + 1) * SHARE]
+        for o in range(first, min(end, OWNERS - 1)):
+            copy = pltpu.make_async_remote_copy(
+                src_ref=part.at[o],
+                dst_ref=arrived.at[o],
+                send_sem=sum_send.at[o],
+                recv_sem=sum_recv.at[o],
+                device_id=(t, owner(o)),
+                device_id_type=MESH,
+            )
+            copy.start()
+            sum_copies.append(copy)
+    beam = part[OWNERS - 1]
+    for o in range(OWNERS - 1):
+        sum_copies[o].wait_recv()
+        beam += arrived[o]
     squares = beam * beam
     folded = squares[0:8] + squares[8:16] + squares[16:24] + squares[24:32]
     final[t] = jnp.sum(folded, axis=0, keepdims=True)

time: 37.1 us -> 35.1 us (0.946)
  Pallas kernels: 36.4 us -> 34.4 us
    pallas_call x1, Pallas kernels: 36.4 us -> 34.4 us  [local(): pl.pallas_call(kernel, out_shape=pltpu.VMEM((GROUP, SHARE), F32), in_spec...]
where the time goes in v3:
time: 35.1 us; the launch traced here: 35 us
  Pallas kernels  34.4 us (98%)
  local copies, waits for them, and re-layouts  0.6 us (2%)
    pallas_call x1, Pallas kernels, local(): pl.pallas_call(kernel, out_shape=pltpu.VMEM((GROUP, SHARE), F32), in_spec...  34.4 us

profile of v3, /device:TPU:1, one launch (start us, length us, event | category | flops | bytes accessed | tf_op | source)
XLA Modules:
  0.0 35.0 jit_solution(776140991876984092)
XLA Ops:
  0.0 34.4 %shard_map.46 = f32[8,128]{1,0:T(8,128)S(1)} custom-call(bf16[4096,512]{1,0:T(8,128)(2,1)} %sig_hbm.1, s32[3,512]{1,0:T(4,128)} %mic_hbm.1, s32[3,8192]{1,0:T(4,128)} %grid_hbm.1, s32[2]{0:T(128)} %bins_hbm.1), custom_call_target="tpu_custom_call" | custom-call | tf_op jit(solution)/shard_map/pallas_call | solution.py:337
  34.4 0.6 %copy.6 = f32[1024]{0:T(1024)} copy(f32[1024]{0:T(1024)S(1)} %bitcast.1) | data formatting | bytes 8192

commit v4 on v3

--- a/solution.py
+++ b/solution.py
@@ -28,7 +28,7 @@
 PAIR = 2 * SHARE
 TILES = LOCAL_MICS // TILE
 STEPS = TILES * OWNERS // 2
-PORTIONS = ((0, 6), (6, 8))
+PORTIONS = ((0, 2), (2, 6), (6, 8))
 
 UNIT = 544.5
 SINE = (-0.020778089505148072, 0.22160904131003262, -0.7069151550432146, 1.0)
@@ -217,38 +217,36 @@
         for copy in lead_copies:
             copy.start()
 
-    group_copies = []
     for m in (7, 6, 3, 2, 5, 4, 1):
         copy = pltpu.make_async_remote_copy(
             src_ref=halves.at[g],
             dst_ref=halves.at[g],
-            send_sem=group_send.at[m],
-            recv_sem=group_recv.at[m],
+            send_sem=group_send,
+            recv_sem=group_recv,
             device_id=(member(m), j),
             device_id_type=MESH,
         )
         copy.start()
-        group_copies.append(copy)
     for d in (-2, 2):
         pl.semaphore_signal(far_sem.at[0], inc=1, device_id=(column(d), j), device_id_type=MESH)
 
-    ready = PORTIONS[0][1] // 2 * TILES
-    lax.fori_loop(CHUNKS, ready, steer, 0)
+    ready = PORTIONS[-1][0] // 2 * TILES
+    lax.fori_loop(CHUNKS, ready, steer, 0, unroll=2)
 
     pl.semaphore_wait(far_sem.at[0], 2)
     for m in range(1, GROUP):
         pl.semaphore_signal(far_sem.at[1], inc=1, device_id=(member(m), j), device_id_type=MESH)
 
-    for m in (1, 4, 5, 2, 3, 6, 7):
-        slot = halves.at[flip(g, 3, m)]
-        pltpu.make_async_remote_copy(
-            src_ref=slot,
-            dst_ref=slot,
-            send_sem=group_send.at[m],
-            recv_sem=group_recv.at[m],
-            device_id=(member(m), j),
-            device_id_type=MESH,
-        ).wait_recv()
+    slots = halves.at[pl.ds(0, GROUP - 1)]
+    members = pltpu.make_async_remote_copy(
+        src_ref=slots,
+        dst_ref=slots,
+        send_sem=group_send,
+        recv_sem=group_recv,
+        device_id=(member(1), j),
+        device_id_type=MESH,
+    )
+    members.wait_recv()
     lead_copies[0].wait_recv()
 
     for s in range(GROUP):
@@ -268,8 +266,8 @@
 
     sum_copies = []
     for first, end in PORTIONS:
-        if first:
-            lax.fori_loop(first // 2 * TILES, end // 2 * TILES, steer, 0)
+        if end == OWNERS:
+            lax.fori_loop(first // 2 * TILES, end // 2 * TILES, steer, 0, unroll=2)
         lanes = slice(first * SHARE, end * SHARE)
         for b in range(NBINS):
             beam = jnp.dot(x_ref[b], w_ref[b, :, lanes], preferred_element_type=F32)
@@ -310,7 +308,8 @@
         for copy in lead_copies:
             copy.wait_send()
 
-    for copy in group_copies + sum_copies:
+    members.wait_send()
+    for copy in sum_copies:
         copy.wait_send()
     others = final.at[pl.ds(0, SPANS - 1)]
     rest = pltpu.make_async_remote_copy(
@@ -358,8 +357,8 @@
             dma((3,)),
             dma((GROUP,)),
             dma,
-            dma((GROUP,)),
-            dma((GROUP,)),
+            dma,
+            dma,
             dma((OWNERS,)),
             dma((OWNERS,)),
             dma,

time: 35.1 us -> 34.8 us (level)
  Pallas kernels: 34.4 us -> 34 us
    pallas_call x1, Pallas kernels: 34.4 us -> 34 us  [local(): pl.pallas_call(kernel, out_shape=pltpu.VMEM((GROUP, SHARE), F32), in_spec...]
where the time goes in v4:
time: 34.8 us; the launch traced here: 34.6 us
  Pallas kernels  34 us (98%)
  local copies, waits for them, and re-layouts  0.6 us (2%)
    pallas_call x1, Pallas kernels, local(): pl.pallas_call(kernel, out_shape=pltpu.VMEM((GROUP, SHARE), F32), in_spec...  34 us

profile of v4, /device:TPU:1, one launch (start us, length us, event | category | flops | bytes accessed | tf_op | source)
XLA Modules:
  0.0 34.6 jit_solution(11462943394436663987)
XLA Ops:
  0.0 34.0 %shard_map.46 = f32[8,128]{1,0:T(8,128)S(1)} custom-call(bf16[4096,512]{1,0:T(8,128)(2,1)} %sig_hbm.1, s32[3,512]{1,0:T(4,128)} %mic_hbm.1, s32[3,8192]{1,0:T(4,128)} %grid_hbm.1, s32[2]{0:T(128)} %bins_hbm.1), custom_call_target="tpu_custom_call" | custom-call | tf_op jit(solution)/shard_map/pallas_call | solution.py:336
  34.1 0.6 %copy.6 = f32[1024]{0:T(1024)} copy(f32[1024]{0:T(1024)S(1)} %bitcast.1) | data formatting | bytes 8192
